TPU v7x, 32 devices: a whole 2x2x4 slice. The times are simulated.
32 devices in a mesh: groups: 2 (over y), wide: 4 (over z), narrow: 4 (over x, core).
Axes of the slice: x: 2, y: 2, z: 4, core: 2. Of those that a mesh axis runs over, the one named last changes fastest.
Arguments:
- inputs: bfloat16 [2, 64, 16384], P(None, 'groups', 'wide'), parts along dimension 1, may hold values from -6 to 6
- w_qkv: bfloat16 [16384, 14336], P('wide', 'narrow'), may hold values from -0.046875 to 0.046875
- w_out: bfloat16 [12288, 16384], P('narrow', 'wide'), may hold values from -0.21875 to 0.21875
- key_cache: bfloat16 [64, 8, 256, 128], P(('groups', 'wide'), 'narrow'), parts along dimension 0, may hold values from -9 to 9
- value_cache: bfloat16 [64, 8, 256, 128], P(('groups', 'wide'), 'narrow'), parts along dimension 0, may hold values from -6 to 6
- positions: int32 [64], P(('groups', 'wide')), parts along dimension 0, may hold values from 0 to 8191
- lengths: int32 [64], P(('groups', 'wide')), parts along dimension 0, may hold values from 1 to 256, as said below
Outputs:
- attended: bfloat16 [2, 64, 16384], P(None, ('groups', 'narrow'), 'wide'), parts along dimension 1
There are 2 independent parts, one for each index of `groups`. A program takes and returns all parts, laid end to end along the dimension named above; an argument that names none is the same for every part. Nothing has to cross between parts.
Inputs may be any that keep to these rules, and one draw needn't show every extreme that they name: `lengths`: at least one row has all 256 slots valid.
All inputs are finite; a program needn't handle non-finite values.
Results may differ from a plain program's by a relative error of at most 0.025.
Values may be sent and summed in bfloat16 or wider, within the bound.
A program may use at most 128 MiB of HBM per device.

v0:
```python
import functools

import jax
import jax.numpy as jnp
import numpy as np
from jax import lax
from jax.experimental import pallas as pl
from jax.experimental.pallas import tpu as pltpu
from jax.sharding import PartitionSpec as P

MESH = pl.DeviceIdType.MESH
F32 = jnp.float32
BF16 = jnp.bfloat16


def layer_kernel(
    s,
    pos_ref, len_ref, freq_ref, x_hbm, wq_hbm, wo_hbm, kc_hbm, vc_hbm,
    out_ref,
    x_v, wq_v, wo_v, kc_v, vc_v,
    qsend, qrecv, heads_v, acc, psend, precv, qs, os,
    x_sem, kv_sem, wq_sem, wo_sem,
    qsend_sem, qrecv_sem, gsend_sem, grecv_sem, psend_sem, precv_sem,
):
    nw, nn = s["nw"], s["nn"]
    H, G, HD = s["H"], s["G"], s["HD"]
    R = s["R"]
    C, NC, B = s["C"], s["NC"], s["B"]
    C2, NP = s["C2"], s["NP"]
    HK = G * HD
    GP = s["GP"]
    slots = s["slots"]
    q = nw // nn
    total = H * NC
    pieces = H * NP
    scale = HD ** -0.5
    me = lax.axis_index("wide")
    me_n = lax.axis_index("narrow")

    def wide_at(d):
        return lax.rem(me + d, nw)

    def narrow_at(d):
        return lax.rem(me_n + d, nn)

    def wq_copy(i):
        slot = lax.rem(i, B)
        return pltpu.make_async_copy(
            wq_hbm.at[:, pl.ds(pl.multiple_of(i * C, C), C)], wq_v.at[slot], wq_sem.at[slot]
        )

    def wo_copy(i):
        h, c = i // NP, lax.rem(i, NP)
        return pltpu.make_async_copy(
            wo_hbm.at[pl.ds(pl.multiple_of(h * HK, HK), HK), pl.ds(pl.multiple_of(c * C2, C2), C2)],
            wo_v.at[i],
            wo_sem.at[i],
        )

    x_copy = pltpu.make_async_copy(x_hbm, x_v, x_sem)
    k_copy = pltpu.make_async_copy(kc_hbm, kc_v, kv_sem.at[0])
    v_copy = pltpu.make_async_copy(vc_hbm, vc_v, kv_sem.at[1])
    x_copy.start()
    for i in range(B):
        wq_copy(jnp.int32(i)).start()
    k_copy.start()
    v_copy.start()

    barrier = pltpu.get_barrier_semaphore()
    for d in range(1, nw):
        pl.semaphore_signal(barrier, inc=1, device_id={"wide": wide_at(d)}, device_id_type=MESH)
    for d in range(1, nn):
        pl.semaphore_signal(barrier, inc=1, device_id={"narrow": narrow_at(d)}, device_id_type=MESH)

    row_id = lax.broadcasted_iota(jnp.int32, (R, HD), 0)
    place = jnp.zeros((R, HD), jnp.int32)
    for r in range(R):
        place = jnp.where(row_id == r, pos_ref[r], place)
    freq = jnp.broadcast_to(freq_ref[...], (R, HD))
    lane = lax.broadcasted_iota(jnp.int32, (2 * R, HD), 1)
    angles = jnp.concatenate([place.astype(F32) * freq, (place + 1).astype(F32) * freq], axis=0)
    cosine = jnp.cos(angles)
    sine = jnp.sin(angles)
    sine = jnp.where(lane < HD // 2, -sine, sine)
    qs[...] = jnp.zeros_like(qs)

    pl.semaphore_wait(barrier, nw + nn - 2)
    x_copy.wait()

    def chunk(i, h):
        c = i - h * NC
        wq_copy(i).wait()
        slot = lax.rem(i, B)
        got = jnp.dot(
            x_v[...].reshape(2 * nw * R, x_v.shape[-1]), wq_v[slot], preferred_element_type=F32
        )
        half = nw * R
        for p in range(nw):
            qsend[h, p, c] = jnp.concatenate(
                [got[p * R:(p + 1) * R], got[half + p * R:half + (p + 1) * R]], axis=0
            ).astype(BF16)
        for d in range(1, nw):
            to = wide_at(d)
            pltpu.make_async_remote_copy(
                src_ref=qsend.at[h, to, c],
                dst_ref=qrecv.at[h, me, c],
                send_sem=qsend_sem.at[h, d],
                recv_sem=qrecv_sem.at[h, d],
                device_id={"wide": to},
                device_id_type=MESH,
            ).start()

        @pl.when(i + B < total)
        def _():
            wq_copy(i + B).start()

        @pl.when((i + B >= total) & (i + B - total < pieces))
        def _():
            wo_copy(i + B - total).start()

    def chunks(h, lo, hi):
        def body(i, carry):
            chunk(i, h)
            return carry

        lax.fori_loop(h * NC + lo, h * NC + hi, body, 0)

    def attention(h):
        joined = qsend[h, me].astype(F32)
        for d in range(1, nw):
            src = lax.rem(me + nw - d, nw)
            pltpu.make_async_copy(qrecv.at[h, src], qrecv.at[h, src], qrecv_sem.at[h, d]).wait()
            joined = joined + qrecv[h, src].astype(F32)
        per = C // HD

        def entry(g):
            return joined[g // per][:, (g % per) * HD:(g % per + 1) * HD]

        def rotated(g):
            t = entry(g)
            t = t * cosine + pltpu.roll(t, HD // 2, 1) * sine
            return t.astype(BF16).astype(F32)

        for g in range(G):
            t = rotated(g)
            qs[:, g, :] = t[:R]
            qs[:, GP + g, :] = t[R:]
        key_new = rotated(G)
        value_new = entry(G + 1).astype(BF16).astype(F32)
        slot_id = lax.broadcasted_iota(jnp.int32, (2 * GP, slots), 1)
        second = lax.broadcasted_iota(jnp.int32, (2 * GP, 1), 0) >= GP
        for r in range(R):
            qr = qs[r]
            scores = lax.dot_general(
                qr.astype(BF16), kc_v[r, h], (((1,), (1,)), ((), ())), preferred_element_type=F32
            ) * scale
            e = jnp.where(slot_id < len_ref[r], jnp.exp(scores), 0.0)
            f0 = jnp.exp(jnp.sum(qr * key_new[r:r + 1], axis=1, keepdims=True) * scale)
            f1 = jnp.exp(jnp.sum(qr * key_new[R + r:R + r + 1], axis=1, keepdims=True) * scale)
            f1 = jnp.where(second, f1, 0.0)
            den = jnp.sum(e, axis=1, keepdims=True) + f0 + f1
            o = jnp.dot((e / den).astype(BF16), vc_v[r, h], preferred_element_type=F32)
            o = o + (f0 / den).astype(BF16).astype(F32) * value_new[r:r + 1]
            o = o + (f1 / den).astype(BF16).astype(F32) * value_new[R + r:R + r + 1]
            os[r] = o
        for g in range(G):
            heads_v[h, me, :, g * HD:(g + 1) * HD] = jnp.concatenate(
                [os[:, g, :], os[:, GP + g, :]], axis=0
            ).astype(BF16)
        for d in range(1, nw):
            pltpu.make_async_remote_copy(
                src_ref=heads_v.at[h, me],
                dst_ref=heads_v.at[h, me],
                send_sem=gsend_sem.at[h, d],
                recv_sem=grecv_sem.at[h, d],
                device_id={"wide": wide_at(d)},
                device_id_type=MESH,
            ).start()

    def project(h):
        for d in range(1, nw):
            src = lax.rem(me + nw - d, nw)
            pltpu.make_async_copy(heads_v.at[h, src], heads_v.at[h, src], grecv_sem.at[h, d]).wait()

        def body(c, carry):
            i = h * NP + c
            wo_copy(i).wait()
            got = jnp.dot(
                heads_v[h].reshape(nw * 2 * R, HK), wo_v[i], preferred_element_type=F32
            )
            if h > 0:
                got = got + acc[c]
            if h < H - 1:
                acc[c] = got
                return carry
            rows = q * 2 * R
            for n in range(nn):
                psend[n, c] = got[n * rows:(n + 1) * rows].astype(BF16)
            for d in range(1, nn):
                to = narrow_at(d)
                pltpu.make_async_remote_copy(
                    src_ref=psend.at[to, c],
                    dst_ref=precv.at[me_n, c],
                    send_sem=psend_sem.at[d],
                    recv_sem=precv_sem.at[d],
                    device_id={"narrow": to},
                    device_id_type=MESH,
                ).start()
            return carry

        lax.fori_loop(0, NP, body, 0)

    for h in range(H):
        cut = (NC + 1) // 2 if h > 0 else NC
        chunks(h, 0, cut)
        if h > 0:
            if h == 1:
                k_copy.wait()
                v_copy.wait()
            attention(h - 1)
            chunks(h, cut, NC)
    if H == 1:
        k_copy.wait()
        v_copy.wait()
    for i in range(min(B, pieces), pieces):
        wo_copy(jnp.int32(i)).start()
    attention(H - 1)
    for h in range(H):
        project(h)

    for d in range(1, nn):
        src = lax.rem(me_n + nn - d, nn)
        pltpu.make_async_copy(precv.at[src], precv.at[src], precv_sem.at[d]).wait()
    for c in range(NP):
        tot = psend[me_n, c].astype(F32)
        for d in range(1, nn):
            tot = tot + precv[narrow_at(d), c].astype(F32)
        for t in range(2):
            part = jnp.concatenate(
                [tot[(2 * k + t) * R:(2 * k + t + 1) * R] for k in range(q)], axis=0
            )
            out_ref[t, :, c * C2:(c + 1) * C2] = part.astype(BF16)

    for d in range(1, nw):
        for h in range(H):
            to = wide_at(d)
            pltpu.make_async_copy(qsend.at[h, to], qsend.at[h, to], qsend_sem.at[h, d]).wait()
            pltpu.make_async_copy(heads_v.at[h, me], heads_v.at[h, me], gsend_sem.at[h, d]).wait()
    for d in range(1, nn):
        to = narrow_at(d)
        pltpu.make_async_copy(psend.at[to], psend.at[to], psend_sem.at[d]).wait()


def on_device(nw, nn, inputs, w_qkv, w_out, key_cache, value_cache, positions, lengths):
    R, H, slots, HD = key_cache.shape
    G = w_qkv.shape[1] // (H * HD) - 2
    K = w_qkv.shape[0]
    N = w_out.shape[1]
    HK = G * HD
    C = 2 * HD
    NC = w_qkv.shape[1] // (H * C)
    C2 = min(N, 4 * HD)
    NP = N // C2
    B = min(8, H * NC)
    GP = -(-G // 8) * 8
    q = nw // nn
    s = dict(nw=nw, nn=nn, H=H, G=G, HD=HD, R=R, C=C, NC=NC, B=B, C2=C2, NP=NP, GP=GP, slots=slots)
    half = np.arange(HD // 2, dtype=np.float64)
    freq = (500000.0 ** (-2.0 * half / HD)).astype(np.float32)
    freq = jnp.asarray(np.concatenate([freq, freq])[None, :])
    rows = q * 2 * R
    any_spec = pl.BlockSpec(memory_space=pl.ANY)
    smem = pl.BlockSpec(memory_space=pltpu.SMEM)
    vmem = pl.BlockSpec(memory_space=pltpu.VMEM)
    dma = pltpu.SemaphoreType.DMA
    return pl.pallas_call(
        functools.partial(layer_kernel, s),
        out_shape=jax.ShapeDtypeStruct((2, q * R, N), BF16),
        in_specs=[smem, smem, vmem] + [any_spec] * 5,
        out_specs=vmem,
        scratch_shapes=[
            pltpu.VMEM(inputs.shape, BF16),
            pltpu.VMEM((B, K, C), BF16),
            pltpu.VMEM((H * NP, HK, C2), BF16),
            pltpu.VMEM(key_cache.shape, BF16),
            pltpu.VMEM(value_cache.shape, BF16),
            pltpu.VMEM((H, nw, NC, 2 * R, C), BF16),
            pltpu.VMEM((H, nw, NC, 2 * R, C), BF16),
            pltpu.VMEM((H, nw, 2 * R, HK), BF16),
            pltpu.VMEM((NP, nw * 2 * R, C2), F32),
            pltpu.VMEM((nn, NP, rows, C2), BF16),
            pltpu.VMEM((nn, NP, rows, C2), BF16),
            pltpu.VMEM((R, 2 * GP, HD), F32),
            pltpu.VMEM((R, 2 * GP, HD), F32),
            dma,
            dma((2,)),
            dma((B,)),
            dma((H * NP,)),
            dma((H, nw)),
            dma((H, nw)),
            dma((H, nw)),
            dma((H, nw)),
            dma((nn,)),
            dma((nn,)),
        ],
        compiler_params=pltpu.CompilerParams(
            collective_id=0, has_side_effects=True, vmem_limit_bytes=58 * 1024 * 1024
        ),
        cost_estimate=pl.CostEstimate(
            flops=4 * nw * R * (K * w_qkv.shape[1] + H * HK * N),
            bytes_accessed=2 * (w_qkv.size + w_out.size + 2 * key_cache.size),
            transcendentals=0,
        ),
    )(positions, lengths, freq, inputs, w_qkv, w_out, key_cache, value_cache)


def solution(mesh):
    placed = (
        P(None, "groups", "wide"),
        P("wide", "narrow"),
        P("narrow", "wide"),
        P(("groups", "wide"), "narrow", None, None),
        P(("groups", "wide"), "narrow", None, None),
        P(("groups", "wide")),
        P(("groups", "wide")),
    )
    return jax.shard_map(
        functools.partial(on_device, mesh.shape["wide"], mesh.shape["narrow"]),
        mesh=mesh,
        in_specs=placed,
        out_specs=P(None, ("groups", "narrow"), "wide"),
        check_vma=False,
    )
```

profile of v0, /device:TPU:0, one launch (start us, length us, event | category | flops | bytes accessed | tf_op | source)
XLA Modules:
  0.0 43.4 jit_solution(14341375029371503714)
XLA Ops:
  0.0 41.8 %shard_map.82 = bf16[2,8,4096]{2,1,0:T(8,128)(2,1)} custom-call(s32[8]{0:T(128)} %pos_ref.1, s32[8]{0:T(128)} %len_ref.1, f32[1,128]{1,0:T(1,128)} %constant.2.clone.freq_ref, bf16[2,32,4096]{2,1,0:T(8,128)(2,1)} %x_hbm.1, bf16[4096,3584]{1,0:T(8,128)(2,1)} %wq_hbm.1, bf16[3072,4096]{1,0:T(8,128)(2,1)} %wo_hbm.1, bf16[8,2,256,128]{3,2,1,0:T(8,128)(2,1)} %kc_hbm.1, ...), custom_call_target="tpu_custom_call" | custom-call | flops 3489660928 | bytes 56623104 | tf_op jit(solution)/shard_map/pallas_call | solution.py:276
  41.8 1.6 %copy.10 = bf16[2,8,4096]{2,1,0:T(8,128)(2,1)} copy(bf16[2,8,4096]{2,1,0:T(8,128)(2,1)} %shard_map.82) | data formatting | bytes 262144
where the time goes:
time: 43.6 us; the launch traced here: 43.4 us
  Pallas kernels  41.8 us (96%)
  local copies, waits for them, and re-layouts  1.57 us (4%)
    pallas_call x1, Pallas kernels, on_device(): pl.pallas_call(functools.partial(layer_kernel, s), out_shape=jax.ShapeDty...  41.8 us
    unnamed x1, local copies, waits for them, and re-layouts  1.57 us

commit v1 on v0

v1 whole, which is shorter than its diff:
```python
import functools

import jax
import jax.numpy as jnp
import numpy as np
from jax import lax
from jax.experimental import pallas as pl
from jax.experimental.pallas import tpu as pltpu
from jax.sharding import PartitionSpec as P

MESH = pl.DeviceIdType.MESH
F32 = jnp.float32
BF16 = jnp.bfloat16


def reversed_bits(p, n):
    out, j = 0, 1
    while j < n:
        out = out * 2 + (p // j) % 2
        j *= 2
    return out


class Halving:
    def __init__(self, axis, n, cur, sends, recvs, send_sem, recv_sem):
        self.axis, self.n, self.cur = axis, n, cur
        self.sends, self.recvs = sends, recvs
        self.send_sem, self.recv_sem = send_sem, recv_sem
        self.stages = len(sends)
        self.me = lax.axis_index(axis)
        self.place = reversed_bits(self.me, n)

    def partner(self, k):
        return self.me + (1 - 2 * ((self.me // 2 ** k) % 2)) * 2 ** k

    def regions(self, k):
        size = self.n // 2 ** (k + 1)
        keep = (self.place // size) * size
        return size, keep, keep + (1 - 2 * ((self.me // 2 ** k) % 2)) * size

    def copy(self, k, i):
        return pltpu.make_async_remote_copy(
            src_ref=self.sends[k].at[i],
            dst_ref=self.recvs[k].at[i],
            send_sem=self.send_sem.at[k, i],
            recv_sem=self.recv_sem.at[k, i],
            device_id={self.axis: self.partner(k)},
            device_id_type=MESH,
        )

    def exchange(self, k, i):
        if k > 0:
            size, keep, _ = self.regions(k - 1)
            self.copy(k - 1, i).wait_recv()
            self.cur[i, pl.ds(keep, size)] += self.recvs[k - 1][i].astype(F32)
        size, _, away = self.regions(k)
        self.sends[k][i] = self.cur[i, pl.ds(away, size)].astype(BF16)
        self.copy(k, i).start()

    def result(self, i):
        self.copy(self.stages - 1, i).wait_recv()
        return self.cur[i, self.place] + self.recvs[-1][i, 0].astype(F32)

    def finish(self, count):
        for k in range(self.stages):
            for i in range(count):
                self.copy(k, i).wait_send()


def layer_kernel(
    s,
    pos_ref, len_ref, freq_ref, x_hbm, wq_hbm, wo_hbm, kc_hbm, vc_hbm,
    out_ref,
    x_v, wq_v, wo_v, kc_v, vc_v,
    qcur, qsend, qrecv, heads_v, acc, psend, precv, qs, os,
    x_sem, kv_sem, wq_sem, wo_sem,
    qsend_sem, qrecv_sem, gsend_sem, grecv_sem, psend_sem, precv_sem,
):
    nw, nn = s["nw"], s["nn"]
    H, G, HD = s["H"], s["G"], s["HD"]
    R = s["R"]
    C, NC, B = s["C"], s["NC"], s["B"]
    C2, NP = s["C2"], s["NP"]
    HK = G * HD
    GP = s["GP"]
    slots = s["slots"]
    q = nw // nn
    total = H * NC
    pieces = H * NP
    scale = HD ** -0.5
    me = lax.axis_index("wide")
    qsum = Halving("wide", nw, qcur, qsend, qrecv, qsend_sem, qrecv_sem)
    psum = Halving("narrow", nn, acc, psend, precv, psend_sem, precv_sem)
    SW, SN, LAG = qsum.stages, psum.stages, 2

    def wq_copy(i):
        slot = lax.rem(i, B)
        return pltpu.make_async_copy(
            wq_hbm.at[:, pl.ds(pl.multiple_of(i * C, C), C)], wq_v.at[slot], wq_sem.at[slot]
        )

    def wo_copy(i):
        h, c = i // NP, lax.rem(i, NP)
        return pltpu.make_async_copy(
            wo_hbm.at[pl.ds(pl.multiple_of(h * HK, HK), HK), pl.ds(pl.multiple_of(c * C2, C2), C2)],
            wo_v.at[i],
            wo_sem.at[i],
        )

    x_copy = pltpu.make_async_copy(x_hbm, x_v, x_sem)
    k_copy = pltpu.make_async_copy(kc_hbm, kc_v, kv_sem.at[0])
    v_copy = pltpu.make_async_copy(vc_hbm, vc_v, kv_sem.at[1])
    x_copy.start()
    for i in range(B):
        wq_copy(jnp.int32(i)).start()
    k_copy.start()
    v_copy.start()

    barrier = pltpu.get_barrier_semaphore()
    for part in (qsum, psum):
        for k in range(part.stages):
            pl.semaphore_signal(
                barrier, inc=1, device_id={part.axis: part.partner(k)}, device_id_type=MESH
            )

    row_id = lax.broadcasted_iota(jnp.int32, (R, HD), 0)
    place = jnp.zeros((R, HD), jnp.int32)
    for r in range(R):
        place = jnp.where(row_id == r, pos_ref[r], place)
    freq = jnp.broadcast_to(freq_ref[...], (R, HD))
    lane = lax.broadcasted_iota(jnp.int32, (2 * R, HD), 1)
    angles = jnp.concatenate([place.astype(F32) * freq, (place + 1).astype(F32) * freq], axis=0)
    cosine = jnp.cos(angles)
    sine = jnp.sin(angles)
    sine = jnp.where(lane < HD // 2, -sine, sine)
    qs[...] = jnp.zeros_like(qs)

    pl.semaphore_wait(barrier, SW + SN)
    x_copy.wait()

    def chunk(i):
        wq_copy(i).wait()
        slot = lax.rem(i, B)
        got = jnp.dot(
            x_v[...].reshape(2 * nw * R, x_v.shape[-1]), wq_v[slot], preferred_element_type=F32
        )
        half = nw * R
        for p in range(nw):
            qcur[i, reversed_bits(p, nw)] = jnp.concatenate(
                [got[p * R:(p + 1) * R], got[half + p * R:half + (p + 1) * R]], axis=0
            )
        qsum.exchange(0, i)

        @pl.when(i + B < total)
        def _():
            wq_copy(i + B).start()

        @pl.when((i + B >= total) & (i + B - total < pieces))
        def _():
            wo_copy(i + B - total).start()

    def chunks(lo, hi):
        def body(i, carry):
            @pl.when(i < total)
            def _():
                chunk(i)

            for k in range(1, SW):

                @pl.when((i >= k * LAG) & (i < total + k * LAG))
                def _():
                    qsum.exchange(k, i - k * LAG)

            return carry

        lax.fori_loop(lo, hi, body, 0)

    def attention(h):
        joined = [qsum.result(h * NC + c) for c in range(NC)]
        per = C // HD

        def entry(g):
            return joined[g // per][:, (g % per) * HD:(g % per + 1) * HD]

        def rotated(g):
            t = entry(g)
            t = t * cosine + pltpu.roll(t, HD // 2, 1) * sine
            return t.astype(BF16).astype(F32)

        for g in range(G):
            t = rotated(g)
            qs[:, g, :] = t[:R]
            qs[:, GP + g, :] = t[R:]
        key_new = rotated(G)
        value_new = entry(G + 1).astype(BF16).astype(F32)
        slot_id = lax.broadcasted_iota(jnp.int32, (2 * GP, slots), 1)
        second = lax.broadcasted_iota(jnp.int32, (2 * GP, 1), 0) >= GP
        for r in range(R):
            qr = qs[r]
            scores = lax.dot_general(
                qr.astype(BF16), kc_v[r, h], (((1,), (1,)), ((), ())), preferred_element_type=F32
            ) * scale
            e = jnp.where(slot_id < len_ref[r], jnp.exp(scores), 0.0)
            f0 = jnp.exp(jnp.sum(qr * key_new[r:r + 1], axis=1, keepdims=True) * scale)
            f1 = jnp.exp(jnp.sum(qr * key_new[R + r:R + r + 1], axis=1, keepdims=True) * scale)
            f1 = jnp.where(second, f1, 0.0)
            den = jnp.sum(e, axis=1, keepdims=True) + f0 + f1
            o = jnp.dot((e / den).astype(BF16), vc_v[r, h], preferred_element_type=F32)
            o = o + (f0 / den).astype(BF16).astype(F32) * value_new[r:r + 1]
            o = o + (f1 / den).astype(BF16).astype(F32) * value_new[R + r:R + r + 1]
            os[r] = o
        for g in range(G):
            heads_v[h, qsum.place, :, g * HD:(g + 1) * HD] = jnp.concatenate(
                [os[:, g, :], os[:, GP + g, :]], axis=0
            ).astype(BF16)
        gather(h, 0)

    def gather_copy(h, j):
        k = SW - 1 - j
        size, keep, _ = qsum.regions(k)
        return pltpu.make_async_remote_copy(
            src_ref=heads_v.at[h, pl.ds(keep, size)],
            dst_ref=heads_v.at[h, pl.ds(keep, size)],
            send_sem=gsend_sem.at[h, j],
            recv_sem=grecv_sem.at[h, j],
            device_id={"wide": qsum.partner(k)},
            device_id_type=MESH,
        )

    def gather_wait(h, j):
        size, _, away = qsum.regions(SW - 1 - j)
        landed = heads_v.at[h, pl.ds(away, size)]
        pltpu.make_async_copy(landed, landed, grecv_sem.at[h, j]).wait()

    def gather(h, j):
        if j > 0:
            gather_wait(h, j - 1)
        gather_copy(h, j).start()

    def project(h, lo, hi):
        def piece(c):
            i = h * NP + c
            wo_copy(i).wait()
            got = jnp.dot(
                heads_v[h].reshape(nw * 2 * R, HK), wo_v[i], preferred_element_type=F32
            )
            for n in range(nn):
                block = jnp.concatenate(
                    [
                        got[reversed_bits(p, nw) * 2 * R:(reversed_bits(p, nw) + 1) * 2 * R]
                        for p in range(n * q, (n + 1) * q)
                    ],
                    axis=0,
                )
                at = reversed_bits(n, nn)
                acc[c, at] = acc[c, at] + block if h > 0 else block
            if h == H - 1:
                psum.exchange(0, c)

        def body(c, carry):
            @pl.when(c < NP)
            def _():
                piece(c)

            if h == H - 1:
                for k in range(1, SN):

                    @pl.when((c >= k * LAG) & (c < NP + k * LAG))
                    def _():
                        psum.exchange(k, c - k * LAG)

            return carry

        lax.fori_loop(lo, hi, body, 0)

    early = LAG * (SW - 1) + 3 <= NC
    done = 0
    end = total + LAG * (SW - 1)
    if early:
        for h in range(1, H):
            upto = h * NC + LAG * (SW - 1) + 3
            chunks(done, upto)
            done = upto
            if h == 1:
                k_copy.wait()
                v_copy.wait()
            attention(h - 1)
    chunks(done, end)
    for i in range(min(B, pieces), pieces):
        wo_copy(jnp.int32(i)).start()
    if not early or H == 1:
        k_copy.wait()
        v_copy.wait()
    for h in range(H - 1):
        if not early:
            attention(h)
        for j in range(1, SW):
            gather(h, j)
    attention(H - 1)
    for h in range(H - 1):
        gather_wait(h, SW - 1)
        mid = NP // 2 if h == H - 2 else NP
        project(h, 0, mid)
    for j in range(1, SW):
        gather(H - 1, j)
    if H > 1:
        project(H - 2, NP // 2, NP)
    gather_wait(H - 1, SW - 1)
    project(H - 1, 0, NP + LAG * (SN - 1))

    for c in range(NP):
        tot = psum.result(c)
        for t in range(2):
            part = jnp.concatenate(
                [tot[(2 * k + t) * R:(2 * k + t + 1) * R] for k in range(q)], axis=0
            )
            out_ref[t, :, c * C2:(c + 1) * C2] = part.astype(BF16)

    qsum.finish(total)
    psum.finish(NP)
    for h in range(H):
        for j in range(SW):
            gather_copy(h, j).wait_send()


def on_device(nw, nn, inputs, w_qkv, w_out, key_cache, value_cache, positions, lengths):
    R, H, slots, HD = key_cache.shape
    G = w_qkv.shape[1] // (H * HD) - 2
    K = w_qkv.shape[0]
    N = w_out.shape[1]
    HK = G * HD
    C = 2 * HD
    NC = w_qkv.shape[1] // (H * C)
    C2 = min(N, 4 * HD)
    NP = N // C2
    B = min(8, H * NC)
    GP = -(-G // 8) * 8
    q = nw // nn
    s = dict(nw=nw, nn=nn, H=H, G=G, HD=HD, R=R, C=C, NC=NC, B=B, C2=C2, NP=NP, GP=GP, slots=slots)
    half = np.arange(HD // 2, dtype=np.float64)
    freq = (500000.0 ** (-2.0 * half / HD)).astype(np.float32)
    freq = jnp.asarray(np.concatenate([freq, freq])[None, :])
    rows = q * 2 * R
    SW, SN = nw.bit_length() - 1, nn.bit_length() - 1
    qbufs = [pltpu.VMEM((H * NC, nw // 2 ** (k + 1), 2 * R, C), BF16) for k in range(SW)]
    pbufs = [pltpu.VMEM((NP, nn // 2 ** (k + 1), rows, C2), BF16) for k in range(SN)]
    any_spec = pl.BlockSpec(memory_space=pl.ANY)
    smem = pl.BlockSpec(memory_space=pltpu.SMEM)
    vmem = pl.BlockSpec(memory_space=pltpu.VMEM)
    dma = pltpu.SemaphoreType.DMA
    return pl.pallas_call(
        functools.partial(layer_kernel, s),
        out_shape=jax.ShapeDtypeStruct((2, q * R, N), BF16),
        in_specs=[smem, smem, vmem] + [any_spec] * 5,
        out_specs=vmem,
        scratch_shapes=[
            pltpu.VMEM(inputs.shape, BF16),
            pltpu.VMEM((B, K, C), BF16),
            pltpu.VMEM((H * NP, HK, C2), BF16),
            pltpu.VMEM(key_cache.shape, BF16),
            pltpu.VMEM(value_cache.shape, BF16),
            pltpu.VMEM((H * NC, nw, 2 * R, C), F32),
            qbufs,
            qbufs,
            pltpu.VMEM((H, nw, 2 * R, HK), BF16),
            pltpu.VMEM((NP, nn, rows, C2), F32),
            pbufs,
            pbufs,
            pltpu.VMEM((R, 2 * GP, HD), F32),
            pltpu.VMEM((R, 2 * GP, HD), F32),
            dma,
            dma((2,)),
            dma((B,)),
            dma((H * NP,)),
            dma((SW, H * NC)),
            dma((SW, H * NC)),
            dma((H, SW)),
            dma((H, SW)),
            dma((SN, NP)),
            dma((SN, NP)),
        ],
        compiler_params=pltpu.CompilerParams(
            collective_id=0, has_side_effects=True, vmem_limit_bytes=58 * 1024 * 1024
        ),
        cost_estimate=pl.CostEstimate(
            flops=4 * nw * R * (K * w_qkv.shape[1] + H * HK * N),
            bytes_accessed=2 * (w_qkv.size + w_out.size + 2 * key_cache.size),
            transcendentals=0,
        ),
    )(positions, lengths, freq, inputs, w_qkv, w_out, key_cache, value_cache)


def solution(mesh):
    placed = (
        P(None, "groups", "wide"),
        P("wide", "narrow"),
        P("narrow", "wide"),
        P(("groups", "wide"), "narrow", None, None),
        P(("groups", "wide"), "narrow", None, None),
        P(("groups", "wide")),
        P(("groups", "wide")),
    )
    return jax.shard_map(
        functools.partial(on_device, mesh.shape["wide"], mesh.shape["narrow"]),
        mesh=mesh,
        in_specs=placed,
        out_specs=P(None, ("groups", "narrow"), "wide"),
        check_vma=False,
    )
```

time: 43.6 us -> 52.6 us (1.21)
  Pallas kernels: 41.8 us -> 50.9 us
    pallas_call x1, Pallas kernels: 41.8 us -> 50.9 us  [on_device(): pl.pallas_call(functools.partial(layer_kernel, s), out_shape=jax.ShapeDty...]
where the time goes in v1:
time: 52.6 us; the launch traced here: 52.4 us
  Pallas kernels  50.9 us (97%)
  local copies, waits for them, and re-layouts  1.57 us (3%)
    pallas_call x1, Pallas kernels, on_device(): pl.pallas_call(functools.partial(layer_kernel, s), out_shape=jax.ShapeDty...  50.9 us
    unnamed x1, local copies, waits for them, and re-layouts  1.57 us

profile of v1, /device:TPU:0, one launch (start us, length us, event | category | flops | bytes accessed | tf_op | source)
XLA Modules:
  0.0 52.4 jit_solution(14379593627336435310)
XLA Ops:
  0.0 50.9 %shard_map.82 = bf16[2,8,4096]{2,1,0:T(8,128)(2,1)} custom-call(s32[8]{0:T(128)} %pos_ref.1, s32[8]{0:T(128)} %len_ref.1, f32[1,128]{1,0:T(1,128)} %constant.2.clone.freq_ref, bf16[2,32,4096]{2,1,0:T(8,128)(2,1)} %x_hbm.1, bf16[4096,3584]{1,0:T(8,128)(2,1)} %wq_hbm.1, bf16[3072,4096]{1,0:T(8,128)(2,1)} %wo_hbm.1, bf16[8,2,256,128]{3,2,1,0:T(8,128)(2,1)} %kc_hbm.1, ...), custom_call_target="tpu_custom_call" | custom-call | flops 3489660928 | bytes 56623104 | tf_op jit(solution)/shard_map/pallas_call | solution.py:351
  50.9 1.6 %copy.10 = bf16[2,8,4096]{2,1,0:T(8,128)(2,1)} copy(bf16[2,8,4096]{2,1,0:T(8,128)(2,1)} %shard_map.82) | data formatting | bytes 262144

commit v2 on v0

--- a/solution.py
+++ b/solution.py
@@ -99,7 +99,7 @@
             qsend[h, p, c] = jnp.concatenate(
                 [got[p * R:(p + 1) * R], got[half + p * R:half + (p + 1) * R]], axis=0
             ).astype(BF16)
-        for d in range(1, nw):
+        for d in range(nw - 1, 0, -1):
             to = wide_at(d)
             pltpu.make_async_remote_copy(
                 src_ref=qsend.at[h, to, c],
@@ -211,7 +211,7 @@
         lax.fori_loop(0, NP, body, 0)
 
     for h in range(H):
-        cut = (NC + 1) // 2 if h > 0 else NC
+        cut = NC
         chunks(h, 0, cut)
         if h > 0:
             if h == 1:

time: 43.6 us -> 40.3 us (0.924)
  Pallas kernels: 41.8 us -> 38.6 us
    pallas_call x1, Pallas kernels: 41.8 us -> 38.6 us  [on_device(): pl.pallas_call(functools.partial(layer_kernel, s), out_shape=jax.ShapeDty...]
where the time goes in v2:
time: 40.3 us; the launch traced here: 40.1 us
  Pallas kernels  38.6 us (96%)
  local copies, waits for them, and re-layouts  1.57 us (4%)
    pallas_call x1, Pallas kernels, on_device(): pl.pallas_call(functools.partial(layer_kernel, s), out_shape=jax.ShapeDty...  38.6 us
    unnamed x1, local copies, waits for them, and re-layouts  1.57 us

profile of v2, /device:TPU:0, one launch (start us, length us, event | category | flops | bytes accessed | tf_op | source)
XLA Modules:
  0.0 40.1 jit_solution(15863227704804780474)
XLA Ops:
  0.0 38.6 %shard_map.82 = bf16[2,8,4096]{2,1,0:T(8,128)(2,1)} custom-call(s32[8]{0:T(128)} %pos_ref.1, s32[8]{0:T(128)} %len_ref.1, f32[1,128]{1,0:T(1,128)} %constant.2.clone.freq_ref, bf16[2,32,4096]{2,1,0:T(8,128)(2,1)} %x_hbm.1, bf16[4096,3584]{1,0:T(8,128)(2,1)} %wq_hbm.1, bf16[3072,4096]{1,0:T(8,128)(2,1)} %wo_hbm.1, bf16[8,2,256,128]{3,2,1,0:T(8,128)(2,1)} %kc_hbm.1, ...), custom_call_target="tpu_custom_call" | custom-call | flops 3489660928 | bytes 56623104 | tf_op jit(solution)/shard_map/pallas_call | solution.py:276
  38.6 1.6 %copy.10 = bf16[2,8,4096]{2,1,0:T(8,128)(2,1)} copy(bf16[2,8,4096]{2,1,0:T(8,128)(2,1)} %shard_map.82) | data formatting | bytes 262144

commit v3 on v2

--- a/solution.py
+++ b/solution.py
@@ -213,6 +213,9 @@
     for h in range(H):
         cut = NC
         chunks(h, 0, cut)
+        if h == H - 1:
+            for i in range(min(B, pieces), pieces):
+                wo_copy(jnp.int32(i)).start()
         if h > 0:
             if h == 1:
                 k_copy.wait()
@@ -222,8 +225,6 @@
     if H == 1:
         k_copy.wait()
         v_copy.wait()
-    for i in range(min(B, pieces), pieces):
-        wo_copy(jnp.int32(i)).start()
     attention(H - 1)
     for h in range(H):
         project(h)
@@ -259,7 +260,7 @@
     HK = G * HD
     C = 2 * HD
     NC = w_qkv.shape[1] // (H * C)
-    C2 = min(N, 4 * HD)
+    C2 = min(N, 8 * HD)
     NP = N // C2
     B = min(8, H * NC)
     GP = -(-G // 8) * 8

time: 40.3 us -> 40.1 us (level)
  no operation moved by 1% of the time
where the time goes in v3:
time: 40.1 us; the launch traced here: 39.9 us
  Pallas kernels  38.3 us (96%)
  local copies, waits for them, and re-layouts  1.57 us (4%)
    pallas_call x1, Pallas kernels, on_device(): pl.pallas_call(functools.partial(layer_kernel, s), out_shape=jax.ShapeDty...  38.3 us
    unnamed x1, local copies, waits for them, and re-layouts  1.57 us

profile of v3, /device:TPU:0, one launch (start us, length us, event | category | flops | bytes accessed | tf_op | source)
XLA Modules:
  0.0 39.9 jit_solution(16535352202548057898)
XLA Ops:
  0.0 38.3 %shard_map.82 = bf16[2,8,4096]{2,1,0:T(8,128)(2,1)} custom-call(s32[8]{0:T(128)} %pos_ref.1, s32[8]{0:T(128)} %len_ref.1, f32[1,128]{1,0:T(1,128)} %constant.2.clone.freq_ref, bf16[2,32,4096]{2,1,0:T(8,128)(2,1)} %x_hbm.1, bf16[4096,3584]{1,0:T(8,128)(2,1)} %wq_hbm.1, bf16[3072,4096]{1,0:T(8,128)(2,1)} %wo_hbm.1, bf16[8,2,256,128]{3,2,1,0:T(8,128)(2,1)} %kc_hbm.1, ...), custom_call_target="tpu_custom_call" | custom-call | flops 3489660928 | bytes 56623104 | tf_op jit(solution)/shard_map/pallas_call | solution.py:277
  38.4 1.6 %copy.10 = bf16[2,8,4096]{2,1,0:T(8,128)(2,1)} copy(bf16[2,8,4096]{2,1,0:T(8,128)(2,1)} %shard_map.82) | data formatting | bytes 262144
